TPU v7x, 32 devices: a whole 2x2x4 slice. The times are simulated.
32 devices in a mesh: row: 4 (over z), col: 8 (over y, x, core).
Axes of the slice: x: 2, y: 2, z: 4, core: 2. Of those that a mesh axis runs over, the one named last changes fastest.
Arguments:
- pair_counts: float32 [32, 32, 2, 128, 128], P(('row', 'col')), may hold values from 0.01 to 30
- tile_index: int32 [32, 32, 2], P(('row', 'col')), may hold values from 0 to 255
- slot_counts: int32 [32, 32], P(('row', 'col')), may hold values from 0 to 2, as said below
- row_totals: int32 [8192], P('row'), may hold values from 1000 to 59999
- col_totals: int32 [16384], P('col'), may hold values from 1000 to 59999
- sketch: bfloat16 [16384, 128], P('col'), may hold values from -0.046875 to 0.046875
Outputs:
- range_rows: bfloat16 [8192, 128], P('row')
- corange: bfloat16 [16384, 128], P('col')
Inputs may be any that keep to these rules, and one draw needn't show every extreme that they name: `slot_counts`: slot counts from a shard to an owner; for some owners every shard fills all 2 slots. `tile_index`: tile positions may repeat; repeated tiles add.
All inputs are finite; a program needn't handle non-finite values.
Results may differ from a plain program's by a relative error of at most 0.001.
The roundings to bfloat16 on the way count: a program that leaves them out, or rounds other values in their place, can miss the bound.
Values may be sent and summed in bfloat16 or wider, within the bound.
A program may use at most 128 MiB of HBM per device.

v0:
```python
import math
import jax
import jax.numpy as jnp
from jax import lax
from jax.sharding import PartitionSpec as P

TILE = 128
RT_DEV = 16
CT_DEV = 16
log_shift = 0.25


def pmi_block(tiles, parked, row_here, col_here, grand):
    ntiles = RT_DEV * CT_DEV
    stack = jnp.zeros((ntiles + 1, TILE, TILE), jnp.float32).at[parked].add(tiles)[:ntiles]
    counts_block = (
        stack.reshape(RT_DEV, CT_DEV, TILE, TILE)
        .transpose(0, 2, 1, 3)
        .reshape(RT_DEV * TILE, CT_DEV * TILE)
    )
    scaled = (
        counts_block
        * grand
        / (row_here.astype(jnp.float32)[:, None] * col_here.astype(jnp.float32)[None, :])
    )
    return jnp.maximum(jnp.log1p(scaled) - log_shift, 0.0).astype(jnp.bfloat16)


def on_device(pair_counts, tile_index, slot_counts, row_totals, col_totals, sketch):
    row_count = lax.axis_size("row")
    slots = lax.broadcasted_iota(jnp.int32, tile_index.shape, 2)
    parked = jnp.where(slots < slot_counts[:, :, None], tile_index, RT_DEV * CT_DEV)
    grand = lax.psum(jnp.sum(row_totals.astype(jnp.float32)), "row")
    arrived, places = (
        lax.all_to_all(pair_counts, ("row", "col"), split_axis=1, concat_axis=0, tiled=True),
        lax.all_to_all(parked, ("row", "col"), split_axis=1, concat_axis=0, tiled=True),
    )
    pmi = pmi_block(
        arrived.reshape(-1, TILE, TILE), places.reshape(-1), row_totals, col_totals, grand
    )
    partial_rows = jnp.dot(pmi, sketch, preferred_element_type=jnp.float32)
    range_rows = lax.psum(partial_rows, "col").astype(jnp.bfloat16)
    partial_cols = lax.dot_general(
        pmi, range_rows, (((0,), (0,)), ((), ())), preferred_element_type=jnp.float32
    )
    col_sums = lax.psum(partial_cols, "row")
    total_rows = pmi.shape[0] * row_count
    corange = (col_sums / math.sqrt(total_rows)).astype(jnp.bfloat16)
    return (range_rows, corange)


def solution(mesh):
    placed = (
        P(("row", "col"), None, None, None, None),
        P(("row", "col"), None, None),
        P(("row", "col"), None),
        P("row"),
        P("col"),
        P("col", None),
    )
    return jax.shard_map(
        on_device,
        mesh=mesh,
        in_specs=placed,
        out_specs=(P("row", None), P("col", None)),
        check_vma=False,
    )
```

profile of v0, /device:TPU:0, one launch (start us, length us, event | category | flops | bytes accessed | tf_op | source)
XLA Modules:
  0.0 312.3 jit_solution(12001681732545011220)
XLA Ops:
  7.2 0.0 copy-start
  7.2 0.7 compare_select_fusion.1
  7.9 0.1 copy.17
  8.0 14.2 %all_to_all.8 = s32[1,32,2]{2,0,1:T(1,128)S(1)} all-to-all(s32[1,32,2]{2,0,1:T(1,128)S(1)} %copy.17), channel_id=1, replica_groups=mesh['row'=4,'col'=8] {'row','col'}, dimensions={1} | all-to-all | bytes 512 | tf_op jit(solution)/shard_map/all_to_all | solution.py:36
  22.3 3.6 %all-to-all-start.1 = ((f32[1,32,2,128,128]{4,3,2,0,1:T(8,128)}), f32[1,32,2,128,128]{4,3,2,0,1:T(8,128)}, u32[]{:S(2)}, u32[]{:S(2)}) async-start(f32[1,32,2,128,128]{4,3,2,0,1:T(8,128)} %bitcast.27), calls=%async_computation.1 | async-start | bytes 8388608 | tf_op jit(solution)/shard_map/all_to_all | solution.py:35
  25.8 0.0 all-reduce.3.cloned.1.call-start
  25.9 1.3 convert_reduce_fusion
  27.2 74.1 %psum.21 = f32[]{:T(128)} all-reduce(f32[]{:T(128)} %convert_reduce_fusion), channel_id=1, replica_groups=mesh['row'=4,'col'=8] {'row'}, use_global_device_ids=true, to_apply=%region_2.3 | all-reduce | flops 1 | bytes 8 | tf_op jit(solution)/shard_map/psum | solution.py:33
  101.3 0.7 convert_element_type.16
  102.0 0.7 convert_element_type.17
  102.7 0.5 broadcast.52
  103.2 0.7 reduce.3
  103.9 0.1 reshape.89
  104.0 16.0 %all-to-all-done.1 = f32[1,32,2,128,128]{4,3,2,0,1:T(8,128)} async-done(((f32[1,32,2,128,128]{4,3,2,0,1:T(8,128)}), f32[1,32,2,128,128]{4,3,2,0,1:T(8,128)}, u32[]{:S(2)}, u32[]{:S(2)}) %all-to-all-start.1) | async-done | bytes 4194336 | tf_op jit(solution)/shard_map/all_to_all | solution.py:35
  120.1 7.9 %broadcast_in_dim.6 = f32[257,128,128]{2,1,0:T(8,128)} broadcast(f32[]{:T(128)} %constant.6.clone.1), dimensions={} | broadcast | bytes 16842756 | tf_op jit(solution)/shard_map/broadcast_in_dim | solution.py:15
  128.0 13.3 %scatter_fusion = f32[257,128,128]{2,1,0:T(8,128)} fusion(f32[257,128,128]{2,1,0:T(8,128)} %broadcast_in_dim.6, s32[64]{0:T(128)S(1)} %fusion.4, f32[64,128,128]{2,1,0:T(8,128)} %bitcast.3), kind=kCustom, calls=%fused_computation | custom fusion | flops 1048576 | bytes 12583168 | tf_op jit(solution)/shard_map/scatter-add | solution.py:15
  141.3 7.2 %slice_multiply_fusion = f32[256,128,128]{2,1,0:T(8,128)S(1)} fusion(f32[257,128,128]{2,1,0:T(8,128)} %scatter_fusion, f32[]{:T(128)} %psum.21), kind=kLoop, calls=%fused_computation.5 | loop fusion | flops 4194304 | bytes 33554436 | tf_op jit(solution)/shard_map/mul | solution.py:22
  148.5 21.4 %copy.19 = f32[16,128,16,128]{3,2,1,0:T(8,128)S(1)} copy(f32[16,128,16,128]{3,1,2,0:T(8,128)S(1)} %bitcast.26) | data formatting | bytes 33554432 | tf_op jit(solution)/shard_map/mul | solution.py:22
  169.9 13.8 %fusion.3 = bf16[2048,2048]{1,0:T(8,128)(2,1)S(1)} fusion(f32[256,8,16,128]{3,2,1,0:T(8,128)S(1)} %bitcast.25, f32[2048]{0:T(1024)S(1)} %convert_element_type.17, f32[2048]{0:T(1024)S(1)} %convert_element_type.16), kind=kLoop, calls=%fused_computation.6 | loop fusion | flops 20971520 | bytes 25182208 | tf_op jit(solution)/shard_map/convert_element_type | solution.py:26
  183.7 0.0 copy-start.1
  183.7 3.2 %copy-done.1 = bf16[2048,2048]{1,0:T(8,128)(2,1)} copy-done((bf16[2048,2048]{1,0:T(8,128)(2,1)}, bf16[2048,2048]{1,0:T(8,128)(2,1)S(1)}, u32[]{:S(2)}) %copy-start.1) | copy-done | bytes 8388632
  187.0 0.0 copy-done
  187.0 2.3 fusion.5
  189.3 51.8 %all-reduce.4 = bf16[2048,128]{1,0:T(8,128)(2,1)S(1)} all-reduce(f32[2048,128]{1,0:T(8,128)S(1)} %fusion.5), channel_id=1, replica_groups=mesh['row'=4,'col'=8] {'col'}, use_global_device_ids=true, to_apply=%region_3.4 | all-reduce | flops 262144 | bytes 1572864 | tf_op jit(solution)/shard_map/psum | solution.py:42
  241.1 0.0 copy-start.2
  241.1 7.0 %fusion.6 = f32[2048,128]{1,0:T(8,128)} fusion(bf16[2048,2048]{1,0:T(8,128)(2,1)} %copy-done.1, bf16[2048,128]{1,0:T(8,128)(2,1)S(1)} %all-reduce.4), kind=kOutput, calls=%fused_computation.13 | convolution fusion | flops 1073741824 | bytes 9961472 | tf_op jit(solution)/shard_map/dot_general | solution.py:43
  248.1 0.0 all-reduce.3.cloned.1.call-update
  248.2 55.2 %all-reduce.3.cloned.1.call-done = f32[2048,128]{1,0:T(8,128)} async-done(((f32[2048,128]{1,0:T(8,128)}), f32[2048,128]{1,0:T(8,128)}) %all-reduce.3.cloned.1.call-update) | async-done | bytes 1048592 | tf_op jit(solution)/shard_map/psum | solution.py:46
  303.4 2.1 multiply_convert_fusion
  305.5 0.0 copy-done.2
  (1 shorter events, 0.0 us)
Async XLA Ops:
  7.2 179.8 %copy-start = (bf16[2048,128]{1,0:T(8,128)(2,1)S(1)}, bf16[2048,128]{1,0:T(8,128)(2,1)}, u32[]{:S(2)}) copy-start(bf16[2048,128]{1,0:T(8,128)(2,1)} %param.11) | copy-start | bytes 1572868
  22.3 97.8 %all-to-all-start.1 = ((f32[1,32,2,128,128]{4,3,2,0,1:T(8,128)}), f32[1,32,2,128,128]{4,3,2,0,1:T(8,128)}, u32[]{:S(2)}, u32[]{:S(2)}) async-start(f32[1,32,2,128,128]{4,3,2,0,1:T(8,128)} %bitcast.27), calls=%async_computation.1 | async-start | bytes 8388608 | tf_op jit(solution)/shard_map/all_to_all | solution.py:35
  25.8 277.5 %all-reduce.3.cloned.1.call-start = ((), (), s32[]{:S(2)}) async-start(), calls=%async_computation.2 | async-start | bytes 2097152 | tf_op jit(solution)/shard_map/psum | solution.py:46
  183.7 3.2 %copy-start.1 = (bf16[2048,2048]{1,0:T(8,128)(2,1)}, bf16[2048,2048]{1,0:T(8,128)(2,1)S(1)}, u32[]{:S(2)}) copy-start(bf16[2048,2048]{1,0:T(8,128)(2,1)S(1)} %fusion.3) | copy-start | bytes 25165828
  241.1 64.4 %copy-start.2 = (bf16[2048,128]{1,0:T(8,128)(2,1)}, bf16[2048,128]{1,0:T(8,128)(2,1)S(1)}, u32[]{:S(2)}) copy-start(bf16[2048,128]{1,0:T(8,128)(2,1)S(1)} %all-reduce.4) | copy-start | bytes 1572868
Sparse Core Ops, SparseCore 0:
  248.3 55.0 all-reduce.2
where the time goes:
time: 313 us; the launch traced here: 312 us
  blocking collectives  140 us (45%)
  waiting for transfers between devices  71.2 us (23%)
  other arithmetic  40.6 us (13%)
  local copies, waits for them, and re-layouts  33.2 us (11%)
  between operations  14.1 us (5%)
  matrix products  9.36 us (3%)
  starting transfers between devices  3.63 us (1%)
    psum x1, blocking collectives, on_device(): grand = lax.psum(jnp.sum(row_totals.astype(jnp.float32)), 'row')  74.1 us
    psum x1, waiting for transfers between devices, on_device(): col_sums = lax.psum(partial_cols, 'row')  55.2 us
    psum x1, blocking collectives, on_device(): range_rows = lax.psum(partial_rows, 'col').astype(jnp.bfloat16)  51.8 us
    mul x1, local copies, waits for them, and re-layouts, pmi_block(): counts_block * grand  21.4 us
    all_to_all x1, waiting for transfers between devices, on_device(): lax.all_to_all(pair_counts, ('row', 'col'), split_axis=1, concat_axis=0,...  16 us
    all_to_all x1, blocking collectives, on_device(): lax.all_to_all(parked, ('row', 'col'), split_axis=1, concat_axis=0, tiled...  14.2 us
    convert_element_type x1, other arithmetic, pmi_block(): return jnp.maximum(jnp.log1p(scaled) - log_shift, 0.0).astype(jnp.bfloat16)  13.8 us
    scatter-add x1, other arithmetic, pmi_block(): jnp.zeros((ntiles + 1, TILE, TILE), jnp.float32).at[parked].add(tiles)  13.3 us
  transfers between devices with their start and end apart: 2, of which 2 were waited for; matrix products, arithmetic and copies ran while one was open for 1% of the time, Pallas kernels for 0%

commit v1 on v0

--- a/solution.py
+++ b/solution.py
@@ -8,6 +8,13 @@
 RT_DEV = 16
 CT_DEV = 16
 log_shift = 0.25
+
+
+def exchange_blocks(x, mesh_axis, split, join):
+    peers = lax.axis_size(mesh_axis)
+    blocks = jnp.stack(jnp.split(x, peers, axis=split), axis=0)
+    blocks = lax.all_to_all(blocks, mesh_axis, split_axis=0, concat_axis=0)
+    return jnp.concatenate(blocks, axis=join)
 
 
 def pmi_block(tiles, parked, row_here, col_here, grand):
@@ -32,7 +39,7 @@
     parked = jnp.where(slots < slot_counts[:, :, None], tile_index, RT_DEV * CT_DEV)
     grand = lax.psum(jnp.sum(row_totals.astype(jnp.float32)), "row")
     arrived, places = (
-        lax.all_to_all(pair_counts, ("row", "col"), split_axis=1, concat_axis=0, tiled=True),
+        exchange_blocks(pair_counts, ("row", "col"), 1, 0),
         lax.all_to_all(parked, ("row", "col"), split_axis=1, concat_axis=0, tiled=True),
     )
     pmi = pmi_block(

time: 313 us -> 358 us (1.14)
  local copies, waits for them, and re-layouts: 33.2 us -> 83.8 us
  blocking collectives: 140 us -> 127 us
  starting transfers between devices: 3.63 us -> 13.3 us
    unnamed x6 -> x41, local copies, waits for them, and re-layouts: 3.23 us -> 51.6 us
    all_to_all x1 -> x0, blocking collectives: 14.2 us -> none  [on_device(): lax.all_to_all(parked, ('row', 'col'), split_axis=1, concat_axis=0, tiled...]
    all_to_all x1 -> x2, starting transfers between devices: 3.58 us -> 13.3 us  [the longest x1 7.3 us: on_device(): lax.all_to_all(parked, ('row', 'col'), split_axis=1, concat_axis=0, tiled...]
    all_to_all x1 -> x2, waiting for transfers between devices: 16 us -> 16.9 us  [the longest x1 16.9 us: exchange_blocks(): blocks = lax.all_to_all(blocks, mesh_axis, split_axis=0, concat_axis=0)]
  transfers between devices with their start and end apart: 2 -> 3, of which waited for: 2 -> 2; matrix products, arithmetic and copies ran while one was open for 1% -> 15% of each run, Pallas kernels for 0% -> 0%
where the time goes in v1:
time: 358 us; the launch traced here: 357 us
  blocking collectives  127 us (35%)
  local copies, waits for them, and re-layouts  83.8 us (23%)
  waiting for transfers between devices  70.8 us (20%)
  other arithmetic  38.5 us (11%)
  between operations  14.2 us (4%)
  starting transfers between devices  13.3 us (4%)
  matrix products  9.36 us (3%)
    psum x1, blocking collectives, on_device(): grand = lax.psum(jnp.sum(row_totals.astype(jnp.float32)), 'row')  75.2 us
    psum x1, waiting for transfers between devices, on_device(): col_sums = lax.psum(partial_cols, 'row')  53.9 us
    psum x1, blocking collectives, on_device(): range_rows = lax.psum(partial_rows, 'col').astype(jnp.bfloat16)  51.9 us
    unnamed x41, local copies, waits for them, and re-layouts  51.6 us
    mul x1, local copies, waits for them, and re-layouts, pmi_block(): counts_block * grand  21.4 us
    all_to_all x1, waiting for transfers between devices, exchange_blocks(): blocks = lax.all_to_all(blocks, mesh_axis, split_axis=0, concat_axis=0)  16.9 us
    convert_element_type x1, other arithmetic, pmi_block(): return jnp.maximum(jnp.log1p(scaled) - log_shift, 0.0).astype(jnp.bfloat16)  13.8 us
    scatter-add x1, other arithmetic, pmi_block(): jnp.zeros((ntiles + 1, TILE, TILE), jnp.float32).at[parked].add(tiles)  13.3 us
  transfers between devices with their start and end apart: 3, of which 2 were waited for; matrix products, arithmetic and copies ran while one was open for 15% of the time, Pallas kernels for 0%

profile of v1, /device:TPU:0, one launch (start us, length us, event | category | flops | bytes accessed | tf_op | source)
XLA Modules:
  0.0 356.9 jit_solution(6709724823019802386)
XLA Ops:
  7.2 0.7 compare_select_fusion.1
  8.6 7.3 %all-to-all-start = ((s32[1,32,2]{2,0,1:T(1,128)}), s32[1,32,2]{2,0,1:T(1,128)S(1)}, u32[]{:S(2)}, u32[]{:S(2)}) async-start(s32[1,32,2]{2,0,1:T(1,128)} %copy.16), calls=%async_computation | async-start | bytes 32768 | tf_op jit(solution)/shard_map/all_to_all | solution.py:43
  15.9 1.6 bitcast_dynamic-update-slice_fusion.31
  17.5 1.6 bitcast_dynamic-update-slice_fusion.30
  19.0 1.6 bitcast_dynamic-update-slice_fusion.29
  20.6 1.6 bitcast_dynamic-update-slice_fusion.28
  22.2 1.6 bitcast_dynamic-update-slice_fusion.27
  23.7 1.5 bitcast_dynamic-update-slice_fusion.26
  25.3 1.6 bitcast_dynamic-update-slice_fusion.25
  26.9 1.6 bitcast_dynamic-update-slice_fusion.24
  28.4 1.6 bitcast_dynamic-update-slice_fusion.23
  30.0 1.6 bitcast_dynamic-update-slice_fusion.22
  31.5 1.6 bitcast_dynamic-update-slice_fusion.21
  33.1 1.6 bitcast_dynamic-update-slice_fusion.20
  34.7 1.6 bitcast_dynamic-update-slice_fusion.19
  36.2 1.6 bitcast_dynamic-update-slice_fusion.18
  37.8 1.6 bitcast_dynamic-update-slice_fusion.17
  39.3 1.6 bitcast_dynamic-update-slice_fusion.16
  40.9 1.6 bitcast_dynamic-update-slice_fusion.15
  42.5 1.6 bitcast_dynamic-update-slice_fusion.14
  44.0 1.6 bitcast_dynamic-update-slice_fusion.13
  45.6 1.6 bitcast_dynamic-update-slice_fusion.12
  47.2 1.6 bitcast_dynamic-update-slice_fusion.11
  48.7 1.6 bitcast_dynamic-update-slice_fusion.10
  50.3 1.6 bitcast_dynamic-update-slice_fusion.9
  51.8 1.6 bitcast_dynamic-update-slice_fusion.8
  53.4 1.6 bitcast_dynamic-update-slice_fusion.7
  55.0 1.6 bitcast_dynamic-update-slice_fusion.6
  56.5 1.6 bitcast_dynamic-update-slice_fusion.5
  58.1 1.6 bitcast_dynamic-update-slice_fusion.4
  59.6 1.5 bitcast_dynamic-update-slice_fusion.3
  61.2 1.6 bitcast_dynamic-update-slice_fusion.2
  62.7 1.5 bitcast_dynamic-update-slice_fusion.1
  64.3 1.6 bitcast_dynamic-update-slice_fusion
  65.9 6.0 %all-to-all-start.1 = ((f32[32,1,1,2,128,128]{5,4,3,2,1,0:T(8,128)}), f32[32,1,1,2,128,128]{5,4,3,2,1,0:T(8,128)}, u32[]{:S(2)}, u32[]{:S(2)}) async-start(f32[32,1,1,2,128,128]{5,4,3,2,1,0:T(8,128)} %bitcast_dynamic-update-slice_fusion), calls=%async_computation.1 | async-start | bytes 8388608 | tf_op jit(solution)/shard_map/all_to_all | solution.py:16
  72.5 75.2 %psum.21 = f32[]{:T(128)} all-reduce(f32[]{:T(128)} %convert_reduce_fusion), channel_id=1, replica_groups=mesh['row'=4,'col'=8] {'row'}, use_global_device_ids=true, to_apply=%region_2.3 | all-reduce | flops 1 | bytes 8 | tf_op jit(solution)/shard_map/psum | solution.py:40
  149.0 16.9 %all-to-all-done.1 = f32[32,1,1,2,128,128]{5,4,3,2,1,0:T(8,128)} async-done(((f32[32,1,1,2,128,128]{5,4,3,2,1,0:T(8,128)}), f32[32,1,1,2,128,128]{5,4,3,2,1,0:T(8,128)}, u32[]{:S(2)}, u32[]{:S(2)}) %all-to-all-start.1) | async-done | bytes 4194336 | tf_op jit(solution)/shard_map/all_to_all | solution.py:16
  165.9 7.9 %broadcast_in_dim.6 = f32[257,128,128]{2,1,0:T(8,128)} broadcast(f32[]{:T(128)} %constant.6.clone.1), dimensions={} | broadcast | bytes 16842756 | tf_op jit(solution)/shard_map/broadcast_in_dim | solution.py:22
  173.8 13.3 %scatter_fusion = f32[257,128,128]{2,1,0:T(8,128)} fusion(f32[257,128,128]{2,1,0:T(8,128)} %broadcast_in_dim.6, s32[64]{0:T(128)S(1)} %fusion.4, f32[64,128,128]{2,1,0:T(8,128)} %bitcast.34), kind=kCustom, calls=%fused_computation | custom fusion | flops 1048576 | bytes 12583168 | tf_op jit(solution)/shard_map/scatter-add | solution.py:22
  187.1 7.2 %slice_multiply_fusion = f32[256,128,128]{2,1,0:T(8,128)S(1)} fusion(f32[257,128,128]{2,1,0:T(8,128)} %scatter_fusion, f32[]{:T(128)} %psum.21), kind=kLoop, calls=%fused_computation.5 | loop fusion | flops 4194304 | bytes 33554436 | tf_op jit(solution)/shard_map/mul | solution.py:29
  194.3 21.4 %copy.17 = f32[16,128,16,128]{3,2,1,0:T(8,128)S(1)} copy(f32[16,128,16,128]{3,1,2,0:T(8,128)S(1)} %bitcast.89) | data formatting | bytes 33554432 | tf_op jit(solution)/shard_map/mul | solution.py:29
  215.7 13.8 %fusion.3 = bf16[2048,2048]{1,0:T(8,128)(2,1)S(1)} fusion(f32[256,8,16,128]{3,2,1,0:T(8,128)S(1)} %bitcast.88, f32[2048]{0:T(1024)S(1)} %convert_element_type.17, f32[2048]{0:T(1024)S(1)} %convert_element_type.16), kind=kLoop, calls=%fused_computation.6 | loop fusion | flops 20971520 | bytes 25182208 | tf_op jit(solution)/shard_map/convert_element_type | solution.py:33
  229.6 3.2 copy-done.1
  232.8 2.3 fusion.5
  235.2 51.9 %all-reduce.4 = bf16[2048,128]{1,0:T(8,128)(2,1)S(1)} all-reduce(f32[2048,128]{1,0:T(8,128)S(1)} %fusion.5), channel_id=1, replica_groups=mesh['row'=4,'col'=8] {'col'}, use_global_device_ids=true, to_apply=%region_3.4 | all-reduce | flops 262144 | bytes 1572864 | tf_op jit(solution)/shard_map/psum | solution.py:49
  287.1 7.0 %fusion.6 = f32[2048,128]{1,0:T(8,128)} fusion(bf16[2048,2048]{1,0:T(8,128)(2,1)} %copy-done.1, bf16[2048,128]{1,0:T(8,128)(2,1)S(1)} %all-reduce.4), kind=kOutput, calls=%fused_computation.45 | convolution fusion | flops 1073741824 | bytes 9961472 | tf_op jit(solution)/shard_map/dot_general | solution.py:50
  294.1 53.9 %all-reduce.3.cloned.1.call-done = f32[2048,128]{1,0:T(8,128)} async-done(((f32[2048,128]{1,0:T(8,128)}), f32[2048,128]{1,0:T(8,128)}) %all-reduce.3.cloned.1.call-update) | async-done | bytes 1048592 | tf_op jit(solution)/shard_map/psum | solution.py:53
  348.0 2.1 multiply_convert_fusion
  (20 shorter events, 2.7 us)
Async XLA Ops:
  7.2 225.7 %copy-start = (bf16[2048,128]{1,0:T(8,128)(2,1)S(1)}, bf16[2048,128]{1,0:T(8,128)(2,1)}, u32[]{:S(2)}) copy-start(bf16[2048,128]{1,0:T(8,128)(2,1)} %param.11) | copy-start | bytes 1572868
  8.6 57.3 %all-to-all-start = ((s32[1,32,2]{2,0,1:T(1,128)}), s32[1,32,2]{2,0,1:T(1,128)S(1)}, u32[]{:S(2)}, u32[]{:S(2)}) async-start(s32[1,32,2]{2,0,1:T(1,128)} %copy.16), calls=%async_computation | async-start | bytes 32768 | tf_op jit(solution)/shard_map/all_to_all | solution.py:43
  65.9 6.0 %copy-start.3 = (s32[2048]{0:T(1024)S(1)}, s32[2048]{0:T(1024)}, u32[]{:S(2)}) copy-start(s32[2048]{0:T(1024)} %param.9) | copy-start | bytes 24580
  65.9 81.8 %copy-start.4 = (s32[2048]{0:T(1024)S(1)}, s32[2048]{0:T(1024)}, u32[]{:S(2)}) copy-start(s32[2048]{0:T(1024)} %param.10) | copy-start | bytes 24580
  65.9 100.1 %all-to-all-start.1 = ((f32[32,1,1,2,128,128]{5,4,3,2,1,0:T(8,128)}), f32[32,1,1,2,128,128]{5,4,3,2,1,0:T(8,128)}, u32[]{:S(2)}, u32[]{:S(2)}) async-start(f32[32,1,1,2,128,128]{5,4,3,2,1,0:T(8,128)} %bitcast_dynamic-update-slice_fusion), calls=%async_computation.1 | async-start | bytes 8388608 | tf_op jit(solution)/shard_map/all_to_all | solution.py:16
  71.8 276.1 %all-reduce.3.cloned.1.call-start = ((), (), s32[]{:S(2)}) async-start(), calls=%async_computation.2 | async-start | bytes 2097152 | tf_op jit(solution)/shard_map/psum | solution.py:53
  229.6 3.2 copy-start.1
  287.1 7.0 %copy-start.2 = (bf16[2048,128]{1,0:T(8,128)(2,1)}, bf16[2048,128]{1,0:T(8,128)(2,1)S(1)}, u32[]{:S(2)}) copy-start(bf16[2048,128]{1,0:T(8,128)(2,1)S(1)} %all-reduce.4) | copy-start | bytes 1572868
Sparse Core Ops, SparseCore 0:
  294.2 53.6 all-reduce.2
